TPU v7x, 32 devices: a whole 2x2x4 slice. The times are simulated.
32 devices in a mesh: row: 2 (over x), col: 16 (over z, y, core).
Axes of the slice: x: 2, y: 2, z: 4, core: 2. Of those that a mesh axis runs over, the one named last changes fastest.
Arguments:
- activations: bfloat16 [32768, 896], P(('row', 'col')), may hold values from -6 to 6
- cotangent: bfloat16 [32768, 896], P(('row', 'col')), may hold values from -6 to 6
- inner_first: bfloat16 [14336, 1792], P('col', 'row'), may hold values from -6 to 6
- inner_second: bfloat16 [1792, 14336], P('row', 'col'), may hold values from -6 to 6
- outer_first: float32 [896, 1792], P('col', 'row'), may hold values from -6 to 6
- momentum_first: float32 [896, 1792], P('col', 'row'), may hold values from -3 to 3
- outer_second: float32 [896, 14336], P('row', 'col'), may hold values from -6 to 6
- momentum_second: float32 [896, 14336], P('row', 'col'), may hold values from -3 to 3
Outputs:
- new_outer_first: float32 [896, 1792], P('col', 'row')
- new_momentum_first: float32 [896, 1792], P('col', 'row')
- new_outer_second: float32 [896, 14336], P('row', 'col')
- new_momentum_second: float32 [896, 14336], P('row', 'col')
- reset_first: bfloat16 [14336, 1792], P('col', 'row')
- reset_second: bfloat16 [1792, 14336], P('row', 'col')
All inputs are finite; a program needn't handle non-finite values.
Results may differ from a plain program's by a relative error of at most 0.003.
Values may be sent and summed in bfloat16 or wider, within the bound.
A program may use at most 64 MiB of HBM per device.

v0:
```python
import jax
import jax.numpy as jnp
from jax import lax
from jax.sharding import PartitionSpec as P

inner_rate = 1.0
outer_rate = 0.7
momentum_coef = 0.9


def nesterov(outer_rows, moment_rows, summed, count):
    pseudo_grad = outer_rows - summed / count
    moment_new = momentum_coef * moment_rows + pseudo_grad
    outer_new = outer_rows - outer_rate * (pseudo_grad + momentum_coef * moment_new)
    return (outer_new, moment_new)


def on_device(
    activations,
    cotangent,
    inner_first,
    inner_second,
    outer_first,
    momentum_first,
    outer_second,
    momentum_second,
):
    width = inner_first.shape[0]
    unit_scale = 1.0 / jnp.sqrt(jnp.float32(width))
    row_count = lax.axis_size("row")
    col_count = lax.axis_size("col")
    rows_second = outer_second.shape[0]
    rows_first = outer_first.shape[0]
    hidden = jnp.dot(activations, inner_first, preferred_element_type=jnp.float32) * unit_scale
    logistic = jax.nn.sigmoid(hidden)
    second_in = (hidden * logistic).astype(jnp.bfloat16)
    backward = (
        lax.dot_general(
            cotangent, inner_second, (((1,), (1,)), ((), ())), preferred_element_type=jnp.float32
        )
        * unit_scale
    )
    first_cot = (backward * logistic * (1.0 + hidden * (1.0 - logistic))).astype(jnp.bfloat16)

    def final_rows(inputs, grads, weight):
        grad_rows = (
            lax.dot_general(
                inputs, grads, (((0,), (0,)), ((), ())), preferred_element_type=jnp.float32
            )
            * unit_scale
        )
        return weight.astype(jnp.float32) - inner_rate * grad_rows

    final_second = final_rows(second_in, cotangent, inner_second)
    summed_second = lax.psum(final_second, "row")
    final_first = final_rows(activations, first_cot, inner_first)
    summed_first = lax.psum(final_first, "col")
    mine_second = lax.dynamic_slice_in_dim(
        summed_second, lax.axis_index("row") * rows_second, rows_second, 0
    )
    mine_first = lax.dynamic_slice_in_dim(
        summed_first, lax.axis_index("col") * rows_first, rows_first, 0
    )
    new_outer_second, new_momentum_second = nesterov(
        outer_second, momentum_second, mine_second, row_count
    )
    new_outer_first, new_momentum_first = nesterov(
        outer_first, momentum_first, mine_first, col_count
    )
    reset_second = lax.all_gather(new_outer_second.astype(jnp.bfloat16), "row", axis=0, tiled=True)
    reset_first = lax.all_gather(new_outer_first.astype(jnp.bfloat16), "col", axis=0, tiled=True)
    return (
        new_outer_first,
        new_momentum_first,
        new_outer_second,
        new_momentum_second,
        reset_first,
        reset_second,
    )


def solution(mesh):
    return jax.shard_map(
        on_device,
        mesh=mesh,
        in_specs=(
            P(("row", "col"), None),
            P(("row", "col"), None),
            P("col", "row"),
            P("row", "col"),
            P("col", "row"),
            P("col", "row"),
            P("row", "col"),
            P("row", "col"),
        ),
        out_specs=(
            P("col", "row"),
            P("col", "row"),
            P("row", "col"),
            P("row", "col"),
            P("col", "row"),
            P("row", "col"),
        ),
        check_vma=False,
    )
```

profile of v0, /device:TPU:0, one launch (start us, length us, event | category | flops | bytes accessed | tf_op | source)
XLA Modules:
  0.0 301.0 jit_solution(9940262707756153435)
XLA Ops:
  7.2 0.0 copy-start
  7.2 0.0 copy-start.1
  7.2 0.0 all-reduce.3.cloned.1.call-start
  7.2 1.4 copy-done
  8.7 5.5 %fusion.7 = f32[1024,896]{1,0:T(8,128)} fusion(bf16[1024,896]{1,0:T(8,128)(2,1)S(1)} %copy-done, bf16[896,896]{1,0:T(8,128)(2,1)} %param.10), kind=kOutput, calls=%fused_computation.18 | convolution fusion | flops 1644167168 | bytes 7110656 | tf_op jit(solution)/shard_map/dot_general | solution.py:34
  14.1 0.0 copy-done.1
  14.1 9.4 %bitcast_subtract_fusion = f32[896,896]{1,0:T(8,128)} fusion(bf16[896,896]{1,0:T(8,128)(2,1)} %param.10, bf16[1024,896]{1,0:T(8,128)(2,1)S(1)} %copy-done, f32[1024,896]{1,0:T(8,128)} %fusion.7, bf16[1024,896]{1,0:T(8,128)(2,1)} %param.9, bf16[896,896]{1,0:T(8,128)(2,1)S(1)} %copy-done.1), kind=kOutput, calls=%fused_computation.3 | convolution fusion | flops 3300835328 | bytes 13762560 | tf_op jit(solution)/shard_map/dot_general | solution.py:47
  23.6 0.0 all-reduce.3.cloned.1.call-update
  23.6 0.0 all-reduce.5.cloned.1.call-start
  23.6 2.3 copy.38
  26.0 7.0 %multiply_subtract_fusion = f32[896,896]{0,1:T(8,128)} fusion(bf16[896,896]{0,1:T(8,128)(2,1)} %copy.38, bf16[1024,896]{1,0:T(8,128)(2,1)} %param.9, f32[1024,896]{1,0:T(8,128)} %fusion.7), kind=kOutput, calls=%fused_computation.4 | convolution fusion | flops 1652080640 | bytes 10321920 | tf_op jit(solution)/shard_map/dot_general | solution.py:47
  33.0 0.0 copy-start.3
  33.0 0.0 all-reduce.5.cloned.1.call-update
  33.0 0.0 all-gather.3.cloned.1.call-start
  33.0 97.6 %all-reduce.3.cloned.1.call-done = f32[896,896]{1,0:T(8,128)} async-done(((f32[896,896]{1,0:T(8,128)}), f32[896,896]{1,0:T(8,128)}) %all-reduce.3.cloned.1.call-update) | async-done | bytes 3211280 | tf_op jit(solution)/shard_map/psum | solution.py:57
  130.7 1.9 fusion.6
  132.6 0.0 all-gather.3.cloned.1.call-update
  132.7 0.0 all-gather.5.cloned.1.call-start
  132.7 0.0 copy-done.3
  132.7 1.8 copy.42
  134.5 2.8 copy.41
  137.3 82.1 %all-reduce.5.cloned.1.call-done = f32[896,896]{0,1:T(8,128)} async-done(((f32[896,896]{0,1:T(8,128)}), f32[896,896]{0,1:T(8,128)}) %all-reduce.5.cloned.1.call-update) | async-done | bytes 3211280 | tf_op jit(solution)/shard_map/psum | solution.py:55
  219.5 5.4 %fusion.5 = (bf16[448,896]{0,1:T(8,128)(2,1)S(1)}, f32[448,896]{0,1:T(8,128)}, f32[448,896]{0,1:T(8,128)}) fusion(f32[448,896]{0,1:T(8,128)} %copy.42, f32[896,896]{0,1:T(8,128)} %all-reduce.5.cloned.1.call-done, s32[]{:T(128)S(6)} %select_n.7, f32[448,896]{0,1:T(8,128)} %copy.41), kind=kLoop, calls=%fused_computation.16 | loop fusion | flops 3612672 | bytes 8830980 | tf_op jit(solution)/shard_map/convert_element_type | solution.py:70
  224.9 1.2 copy.43
  226.1 0.0 all-gather.5.cloned.1.call-update
  226.1 2.7 copy.44
  228.8 2.7 copy.45
  231.4 30.6 %all-gather.3.cloned.1.call-done = bf16[896,896]{1,0:T(8,128)(2,1)} async-done(((bf16[56,896]{1,0:T(8,128)(2,1)}), bf16[896,896]{1,0:T(8,128)(2,1)}) %all-gather.3.cloned.1.call-update) | async-done | bytes 1605648 | tf_op jit(solution)/shard_map/all_gather | solution.py:71
  262.0 28.5 %all-gather.5.cloned.1.call-done = bf16[896,896]{1,0:T(8,128)(2,1)} async-done(((bf16[448,896]{1,0:T(8,128)(2,1)}), bf16[896,896]{1,0:T(8,128)(2,1)}) %all-gather.5.cloned.1.call-update) | async-done | bytes 1605648 | tf_op jit(solution)/shard_map/all_gather | solution.py:70
  290.5 2.8 copy.52
  293.3 0.0 copy-done.2
  293.3 1.2 copy.53
  (1 shorter events, 0.0 us)
Async XLA Ops:
  7.2 1.5 copy-start
  7.2 7.0 %copy-start.1 = (bf16[896,896]{1,0:T(8,128)(2,1)S(1)}, bf16[896,896]{1,0:T(8,128)(2,1)}, u32[]{:S(2)}) copy-start(bf16[896,896]{1,0:T(8,128)(2,1)} %param.11) | copy-start | bytes 4816900
  7.2 123.5 %all-reduce.3.cloned.1.call-start = ((), (), s32[]{:S(2)}) async-start(), calls=%async_computation | async-start | bytes 6422528 | tf_op jit(solution)/shard_map/psum | solution.py:57
  23.6 195.9 %all-reduce.5.cloned.1.call-start = ((), (), s32[]{:S(2)}) async-start(), calls=%async_computation.1 | async-start | bytes 6422528 | tf_op jit(solution)/shard_map/psum | solution.py:55
  33.0 99.7 %copy-start.3 = (f32[448,896]{1,0:T(8,128)S(1)}, f32[448,896]{1,0:T(8,128)}, u32[]{:S(2)}) copy-start(f32[448,896]{1,0:T(8,128)} %param.14) | copy-start | bytes 4816900
  33.0 229.1 %all-gather.3.cloned.1.call-start = ((), (), s32[]{:S(2)}) async-start(), calls=%async_computation.2 | async-start | bytes 1705984 | tf_op jit(solution)/shard_map/all_gather | solution.py:71
  132.7 157.9 %all-gather.5.cloned.1.call-start = ((), (), s32[]{:S(2)}) async-start(), calls=%async_computation.3 | async-start | bytes 2408448 | tf_op jit(solution)/shard_map/all_gather | solution.py:70
  290.5 2.8 copy-start.2
Sparse Core Ops, SparseCore 0:
  23.7 106.9 all-reduce.2
  133.1 86.3 all-reduce.4
  222.2 39.7 all-gather.2
  264.0 26.4 all-gather.4
where the time goes:
time: 301 us
  waiting for transfers between devices  239 us (79%)
  matrix products  21.9 us (7%)
  local copies, waits for them, and re-layouts  18.9 us (6%)
  between operations  13.8 us (5%)
  other arithmetic  7.33 us (2%)
    psum x1, waiting for transfers between devices, on_device(): summed_first = lax.psum(final_first, 'col')  97.6 us
    psum x1, waiting for transfers between devices, on_device(): summed_second = lax.psum(final_second, 'row')  82.1 us
    all_gather x1, waiting for transfers between devices, on_device(): lax.all_gather(new_outer_first.astype(jnp.bfloat16), 'col', axis=0, tiled...  30.6 us
    all_gather x1, waiting for transfers between devices, on_device(): lax.all_gather(new_outer_second.astype(jnp.bfloat16), 'row', axis=0, tile...  28.5 us
    unnamed x15, local copies, waits for them, and re-layouts  17.7 us
    dot_general x2, matrix products, final_rows(): lax.dot_general(inputs, grads, (((0,), (0,)), ((), ())), preferred_elemen...  16.4 us
  transfers between devices with their start and end apart: 4, of which 4 were waited for; matrix products, arithmetic and copies ran while one was open for 9% of the time, Pallas kernels for 0%

commit v1 on v0

--- a/solution.py
+++ b/solution.py
@@ -1,6 +1,11 @@
+import functools
+
 import jax
 import jax.numpy as jnp
+import numpy as np
 from jax import lax
+from jax.experimental import pallas as pl
+from jax.experimental.pallas import tpu as pltpu
 from jax.sharding import PartitionSpec as P
 
 inner_rate = 1.0
@@ -15,7 +20,7 @@
     return (outer_new, moment_new)
 
 
-def on_device(
+def on_device_plain(
     activations,
     cotangent,
     inner_first,
@@ -79,9 +84,516 @@
     )
 
 
+MESH = pl.DeviceIdType.MESH
+LANES = 128
+TOKEN_TILE = 256
+CHUNKS = 4
+F32 = jnp.float32
+BF16 = jnp.bfloat16
+
+
+def pack_piece(piece, padded):
+    rows, width = piece.shape
+    blocks = [piece[:, j * LANES : (j + 1) * LANES] for j in range(width // LANES)]
+    spare = padded - rows * len(blocks)
+    if spare:
+        blocks.append(jnp.zeros((spare, LANES), F32))
+    return jnp.concatenate(blocks, axis=0)
+
+
+def unpack_piece(packed, rows, width):
+    return jnp.concatenate(
+        [packed[j * rows : (j + 1) * rows] for j in range(width // LANES)], axis=1
+    )
+
+
+def outer_step_kernel(
+    x_h,
+    g_h,
+    w1_h,
+    w2_h,
+    o1_h,
+    m1_h,
+    o2_h,
+    m2_h,
+    no1_h,
+    nm1_h,
+    no2_h,
+    nm2_h,
+    r1_h,
+    r2_h,
+    xv,
+    gv,
+    w1v,
+    w2v,
+    o1v,
+    m1v,
+    o2v,
+    m2v,
+    xt,
+    st,
+    dv,
+    fc,
+    f2,
+    fsend,
+    frecv,
+    asend,
+    arecv,
+    f1,
+    r1,
+    s2,
+    r2,
+    own,
+    na,
+    nb,
+    no1,
+    nm1,
+    no2,
+    nm2,
+    rs1,
+    rs2,
+    in_sem,
+    out_sem,
+    out2_sem,
+    rs1_sem,
+    fs_sem,
+    fr_sem,
+    as_sem,
+    ar_sem,
+    c1s_sem,
+    c1r_sem,
+    s2s_sem,
+    s2r_sem,
+    zs_sem,
+    ys_sem,
+    nar_sem,
+    ks_sem,
+    nbr_sem,
+):
+    row = lax.axis_index("row")
+    col = lax.axis_index("col")
+    n_col = lax.axis_size("col")
+    chips = n_col // 2
+    core = lax.rem(col, 2)
+    chip = lax.div(col, 2)
+    side = lax.rem(chip, 2)
+    depth = lax.div(chip, 2)
+    depths = chips // 2
+    width = w1v.shape[0]
+    tokens = xv.shape[0]
+    half = o2v.shape[0]
+    chunk = half // CHUNKS
+    piece = o1v.shape[0]
+    padded = s2.shape[1]
+    scale = float(np.float32(1.0) / np.sqrt(np.float32(width)))
+
+    across = (1 - row, col)
+    sibling = (row, chip * 2 + 1 - core)
+
+    def plane(other_chip):
+        return (row, other_chip * 2 + core)
+
+    loads = {}
+    for i, (name, src, dst) in enumerate(
+        (
+            ("x", x_h, xv),
+            ("w1", w1_h, w1v),
+            ("g", g_h, gv),
+            ("w2", w2_h, w2v),
+            ("o2", o2_h, o2v),
+            ("m2", m2_h, m2v),
+            ("o1", o1_h, o1v),
+            ("m1", m1_h, m1v),
+        )
+    ):
+        loads[name] = pltpu.make_async_copy(src, dst, in_sem.at[i])
+        loads[name].start()
+
+    barrier = pltpu.get_barrier_semaphore()
+    pl.semaphore_signal(barrier, inc=1, device_id=across, device_id_type=MESH)
+    pl.semaphore_signal(barrier, inc=1, device_id=sibling, device_id_type=MESH)
+    for d in range(1, chips):
+        pl.semaphore_signal(
+            barrier, inc=1, device_id=plane(lax.rem(chip + d, chips)), device_id_type=MESH
+        )
+
+    def remote(src, dst, send_sem, recv_sem, device):
+        return pltpu.make_async_remote_copy(
+            src_ref=src,
+            dst_ref=dst,
+            send_sem=send_sem,
+            recv_sem=recv_sem,
+            device_id=device,
+            device_id_type=MESH,
+        )
+
+    loads["x"].wait()
+    loads["w1"].wait()
+
+    def forward(t, carry):
+        at = pl.ds(pl.multiple_of(t * TOKEN_TILE, TOKEN_TILE), TOKEN_TILE)
+        inputs = xv[at, :]
+        hidden = jnp.dot(inputs, w1v[...], preferred_element_type=F32) * scale
+        logistic = jax.nn.sigmoid(hidden)
+        st[:, at] = (hidden * logistic).astype(BF16).T
+        dv[at, :] = logistic * (1.0 + hidden * (1.0 - logistic))
+        xt[:, at] = inputs.T
+        return carry
+
+    lax.fori_loop(0, tokens // TOKEN_TILE, forward, 0)
+    loads["g"].wait()
+    loads["w2"].wait()
+    pl.semaphore_wait(barrier, chips + 1)
+
+    mine = row * half
+    theirs = (1 - row) * half
+
+    def rows_of(base, i):
+        return pl.ds(pl.multiple_of(base + i * chunk, 16), chunk)
+
+    def part(i):
+        return pl.ds(pl.multiple_of(i * chunk, 16), chunk)
+
+    def final_second(base, i):
+        at = rows_of(base, i)
+        grad = jnp.dot(st[at, :], gv[...], preferred_element_type=F32) * scale
+        final = w2v[at, :].astype(F32) - inner_rate * grad
+        f2[at, :] = final
+        return final
+
+    def copy_final(i):
+        return remote(fsend.at[part(i)], frecv.at[part(i)], fs_sem.at[i], fr_sem.at[i], across)
+
+    def copy_partial(i):
+        return remote(asend.at[part(i)], arecv.at[part(i)], as_sem.at[i], ar_sem.at[i], across)
+
+    def send_final(i, carry):
+        fsend[part(i), :] = final_second(theirs, i).astype(BF16)
+        copy_final(i).start()
+        return carry
+
+    lax.fori_loop(0, CHUNKS // 2, send_final, 0)
+
+    def backward(t, carry):
+        at = pl.ds(pl.multiple_of(t * TOKEN_TILE, TOKEN_TILE), TOKEN_TILE)
+        back = (
+            lax.dot_general(
+                gv[at, :], w2v[...], (((1,), (1,)), ((), ())), preferred_element_type=F32
+            )
+            * scale
+        )
+        fc[at, :] = (back * dv[at, :]).astype(BF16)
+        return carry
+
+    lax.fori_loop(0, tokens // TOKEN_TILE, backward, 0)
+
+    def copy_core(t):
+        at = pl.ds(t * 2, 2)
+        return remote(
+            f1.at[1 - core, at], r1.at[at], c1s_sem.at[t], c1r_sem.at[t], sibling
+        )
+
+    def final_first(t, carry):
+        rows = 4 * piece
+        at = pl.ds(pl.multiple_of(t * rows, 16), rows)
+        grad = jnp.dot(xt[at, :], fc[...], preferred_element_type=F32) * scale
+        final = w1v[at, :].astype(F32) - inner_rate * grad
+        for j in range(4):
+            f1[j % 2, t * 2 + j // 2] = final[j * piece : (j + 1) * piece]
+        copy_core(t).start()
+        return carry
+
+    lax.fori_loop(0, chips // 2, final_first, 0)
+    lax.fori_loop(CHUNKS // 2, CHUNKS, send_final, 0)
+
+    def wait_core(t, carry):
+        copy_core(t).wait_recv()
+        return carry
+
+    lax.fori_loop(0, chips // 2, wait_core, 0)
+
+    def copy_sum(d):
+        return remote(
+            s2.at[d], r2.at[chip], s2s_sem.at[d], s2r_sem.at[chip], plane(lax.rem(chip + d, chips))
+        )
+
+    def send_sum(d, carry):
+        owner = lax.rem(chip + d, chips)
+        total = f1[core, owner] + r1[owner]
+        s2[d] = pack_piece(total, padded).astype(BF16)
+        copy_sum(d).start()
+        return carry
+
+    lax.fori_loop(1, chips, send_sum, 0)
+    own[...] = pack_piece(f1[core, chip] + r1[chip], padded)
+
+    loads["o2"].wait()
+    loads["m2"].wait()
+
+    def send_partial(i, carry):
+        final = final_second(mine, i)
+        share, _ = nesterov(o2v[part(i), :], m2v[part(i), :], final, 2)
+        asend[part(i), :] = share.astype(BF16)
+        copy_partial(i).start()
+        return carry
+
+    lax.fori_loop(0, CHUNKS, send_partial, 0)
+
+    def out_second(i):
+        return (
+            pltpu.make_async_copy(no2.at[part(i)], no2_h.at[part(i)], out2_sem.at[0, i]),
+            pltpu.make_async_copy(nm2.at[part(i)], nm2_h.at[part(i)], out2_sem.at[1, i]),
+            pltpu.make_async_copy(
+                rs2.at[rows_of(mine, i)], r2_h.at[rows_of(mine, i)], out2_sem.at[2, i]
+            ),
+        )
+
+    def out_reset(i):
+        at = rows_of(theirs, i)
+        return pltpu.make_async_copy(rs2.at[at], r2_h.at[at], out2_sem.at[3, i])
+
+    def take_final(i, carry):
+        copy_final(i).wait_recv()
+        summed = f2[rows_of(mine, i), :] + frecv[part(i), :].astype(F32)
+        new_outer, new_moment = nesterov(o2v[part(i), :], m2v[part(i), :], summed, 2)
+        no2[part(i), :] = new_outer
+        nm2[part(i), :] = new_moment
+        rs2[rows_of(mine, i), :] = new_outer.astype(BF16)
+        for copy in out_second(i):
+            copy.start()
+        return carry
+
+    lax.fori_loop(0, CHUNKS, take_final, 0)
+
+    loads["o1"].wait()
+    loads["m1"].wait()
+
+    def take_sum(d, carry):
+        source = lax.rem(chip + chips - d, chips)
+        remote(
+            s2.at[d], r2.at[source], s2s_sem.at[d], s2r_sem.at[source], plane(source)
+        ).wait_recv()
+        own[...] += r2[source].astype(F32)
+        return carry
+
+    lax.fori_loop(1, chips, take_sum, 0)
+    summed = unpack_piece(own[...], piece, width)
+    new_outer, new_moment = nesterov(o1v[...], m1v[...], summed, n_col)
+    no1[...] = new_outer
+    nm1[...] = new_moment
+    na[chip] = pack_piece(new_outer, padded).astype(BF16)
+    out_first = (
+        pltpu.make_async_copy(no1, no1_h, out_sem.at[0]),
+        pltpu.make_async_copy(nm1, nm1_h, out_sem.at[1]),
+    )
+
+    def copy_depth(d):
+        other = lax.rem(depth + d, depths) * 2 + side
+        return remote(na.at[chip], na.at[chip], zs_sem.at[d], nar_sem.at[chip], plane(other))
+
+    def copy_side(d):
+        held = lax.rem(depth + d, depths) * 2 + side
+        return remote(
+            na.at[held], na.at[held], ys_sem.at[d], nar_sem.at[held], plane(depth * 2 + 1 - side)
+        )
+
+    def copy_sibling(held):
+        return remote(na.at[held], nb.at[held], ks_sem.at[held], nbr_sem.at[held], sibling)
+
+    def wait_module(held):
+        remote(
+            na.at[held], na.at[held], ys_sem.at[0], nar_sem.at[held], plane(depth * 2 + 1 - side)
+        ).wait_recv()
+
+    for d in range(1, depths):
+        copy_depth(d).start()
+    copy_side(0).start()
+    copy_sibling(chip).start()
+    for copy in out_first:
+        copy.start()
+
+    def take_partial(i, carry):
+        copy_partial(i).wait_recv()
+        at = rows_of(theirs, i)
+        share = (outer_rate * (1.0 + momentum_coef) / 2) * f2[at, :]
+        rs2[at, :] = (arecv[part(i), :].astype(F32) + share).astype(BF16)
+        out_reset(i).start()
+        return carry
+
+    lax.fori_loop(0, 2, take_partial, 0)
+
+    def pass_on(d, carry):
+        held = lax.rem(depth + d, depths) * 2 + side
+        wait_module(held)
+        copy_side(d).start()
+        copy_sibling(held).start()
+        return carry
+
+    lax.fori_loop(1, depths, pass_on, 0)
+    lax.fori_loop(2, CHUNKS - 1, take_partial, 0)
+
+    def pass_core(d, carry):
+        held = lax.rem(depth + d, depths) * 2 + 1 - side
+        wait_module(held)
+        copy_sibling(held).start()
+        return carry
+
+    lax.fori_loop(0, depths, pass_core, 0)
+
+    def out_module(q):
+        at = pl.ds(pl.multiple_of(q * 2 * piece, 16), 2 * piece)
+        return pltpu.make_async_copy(rs1.at[at], r1_h.at[at], rs1_sem.at[q])
+
+    def place(d, carry):
+        q = lax.rem(chip + d, chips)
+        remote(na.at[q], nb.at[q], ks_sem.at[q], nbr_sem.at[q], sibling).wait_recv()
+        here = unpack_piece(na[q].astype(F32), piece, width)
+        there = unpack_piece(nb[q].astype(F32), piece, width)
+        both = jnp.concatenate(
+            [jnp.where(core == 0, here, there), jnp.where(core == 0, there, here)], axis=0
+        )
+        rs1[pl.ds(pl.multiple_of(q * 2 * piece, 16), 2 * piece), :] = both.astype(BF16)
+        out_module(q).start()
+        return carry
+
+    lax.fori_loop(0, chips, place, 0)
+    lax.fori_loop(CHUNKS - 1, CHUNKS, take_partial, 0)
+
+    def drain(i, carry):
+        copy_final(i).wait_send()
+        copy_partial(i).wait_send()
+        for copy in out_second(i):
+            copy.wait()
+        out_reset(i).wait()
+        return carry
+
+    lax.fori_loop(0, CHUNKS, drain, 0)
+
+    def drain_core(t, carry):
+        copy_core(t).wait_send()
+        return carry
+
+    lax.fori_loop(0, chips // 2, drain_core, 0)
+    for copy in out_first:
+        copy.wait()
+    for d in range(1, chips):
+        copy_sum(d).wait_send()
+    for d in range(depths):
+        copy_side(d).wait_send()
+        if d:
+            copy_depth(d).wait_send()
+    for q in range(chips):
+        copy_sibling(q).wait_send()
+        out_module(q).wait()
+
+
+def on_device_fused(
+    activations,
+    cotangent,
+    inner_first,
+    inner_second,
+    outer_first,
+    momentum_first,
+    outer_second,
+    momentum_second,
+):
+    tokens, width = activations.shape
+    piece = outer_first.shape[0]
+    half = outer_second.shape[0]
+    chips = lax.axis_size("col") // 2
+    padded = -(-piece * (width // LANES) // 16) * 16
+    anywhere = pl.BlockSpec(memory_space=pl.ANY)
+    dma = pltpu.SemaphoreType.DMA
+    return pl.pallas_call(
+        outer_step_kernel,
+        out_shape=(
+            jax.ShapeDtypeStruct((piece, width), F32),
+            jax.ShapeDtypeStruct((piece, width), F32),
+            jax.ShapeDtypeStruct((half, width), F32),
+            jax.ShapeDtypeStruct((half, width), F32),
+            jax.ShapeDtypeStruct((width, width), BF16),
+            jax.ShapeDtypeStruct((width, width), BF16),
+        ),
+        in_specs=[anywhere] * 8,
+        out_specs=[anywhere] * 6,
+        scratch_shapes=[
+            pltpu.VMEM((tokens, width), BF16),
+            pltpu.VMEM((tokens, width), BF16),
+            pltpu.VMEM((width, width), BF16),
+            pltpu.VMEM((width, width), BF16),
+            pltpu.VMEM((piece, width), F32),
+            pltpu.VMEM((piece, width), F32),
+            pltpu.VMEM((half, width), F32),
+            pltpu.VMEM((half, width), F32),
+            pltpu.VMEM((width, tokens), BF16),
+            pltpu.VMEM((width, tokens), BF16),
+            pltpu.VMEM((tokens, width), F32),
+            pltpu.VMEM((tokens, width), BF16),
+            pltpu.VMEM((width, width), F32),
+            pltpu.VMEM((half, width), BF16),
+            pltpu.VMEM((half, width), BF16),
+            pltpu.VMEM((half, width), BF16),
+            pltpu.VMEM((half, width), BF16),
+            pltpu.VMEM((2, chips, piece, width), F32),
+            pltpu.VMEM((chips, piece, width), F32),
+            pltpu.VMEM((chips, padded, LANES), BF16),
+            pltpu.VMEM((chips, padded, LANES), BF16),
+            pltpu.VMEM((padded, LANES), F32),
+            pltpu.VMEM((chips, padded, LANES), BF16),
+            pltpu.VMEM((chips, padded, LANES), BF16),
+            pltpu.VMEM((piece, width), F32),
+            pltpu.VMEM((piece, width), F32),
+            pltpu.VMEM((half, width), F32),
+            pltpu.VMEM((half, width), F32),
+            pltpu.VMEM((width, width), BF16),
+            pltpu.VMEM((width, width), BF16),
+            dma((8,)),
+            dma((2,)),
+            dma((4, CHUNKS)),
+            dma((chips,)),
+            dma((CHUNKS,)),
+            dma((CHUNKS,)),
+            dma((CHUNKS,)),
+            dma((CHUNKS,)),
+            dma((chips // 2,)),
+            dma((chips // 2,)),
+            dma((chips,)),
+            dma((chips,)),
+            dma((chips // 2,)),
+            dma((chips // 2,)),
+            dma((chips,)),
+            dma((chips,)),
+            dma((chips,)),
+        ],
+        compiler_params=pltpu.CompilerParams(
+            collective_id=0, has_side_effects=True, vmem_limit_bytes=60 * 1024 * 1024
+        ),
+        cost_estimate=pl.CostEstimate(
+            flops=8 * tokens * width * width,
+            bytes_accessed=17_000_000,
+            transcendentals=tokens * width,
+        ),
+    )(
+        activations,
+        cotangent,
+        inner_first,
+        inner_second,
+        outer_first,
+        momentum_first,
+        outer_second,
+        momentum_second,
+    )
+
+
+def on_device(mesh):
+    if mesh.shape["row"] == 2 and mesh.shape["col"] == 16:
+        return on_device_fused
+    return on_device_plain
+
+
 def solution(mesh):
     return jax.shard_map(
-        on_device,
+        on_device(mesh),
         mesh=mesh,
         in_specs=(
             P(("row", "col"), None),

time: 301 us -> 67.3 us (0.22)
  waiting for transfers between devices: 239 us -> 0 us
  Pallas kernels: 0 us -> 54.4 us
  matrix products: 21.9 us -> 0 us
  between operations: 13.8 us -> 0.65 us
  local copies, waits for them, and re-layouts: 18.9 us -> 11.2 us
  other arithmetic: 7.33 us -> 0 us
    psum x2 -> x0, waiting for transfers between devices: 180 us -> none  [the longest x1 97.6 us: on_device(): summed_first = lax.psum(final_first, 'col')]
    all_gather x2 -> x0, waiting for transfers between devices: 59.1 us -> none  [the longest x1 30.6 us: on_device(): lax.all_gather(new_outer_first.astype(jnp.bfloat16), 'col', axis=0, tiled...]
    pallas_call x0 -> x1, Pallas kernels: none -> 54.4 us  [on_device_fused(): pl.pallas_call(outer_step_kernel, out_shape=(jax.ShapeDtypeStruct((piece,...]
    dot_general x3 -> x0, matrix products: 21.9 us -> none  [the longest x2 16.4 us: final_rows(): lax.dot_general(inputs, grads, (((0,), (0,)), ((), ())), preferred_elemen...]
    convert_element_type x2 -> x0, other arithmetic: 7.33 us -> none  [the longest x1 5.38 us: on_device(): new_outer_second.astype(jnp.bfloat16)]
    unnamed x15 -> x12, local copies, waits for them, and re-layouts: 17.7 us -> 11.2 us
  transfers between devices with their start and end apart: 4 -> 0, of which waited for: 4 -> 0; matrix products, arithmetic and copies ran while one was open for 9% -> 0% of each run, Pallas kernels for 0% -> 0%
where the time goes in v1:
time: 67.3 us; the launch traced here: 66.3 us
  Pallas kernels  54.4 us (81%)
  local copies, waits for them, and re-layouts  11.2 us (17%)
    pallas_call x1, Pallas kernels, on_device_fused(): pl.pallas_call(outer_step_kernel, out_shape=(jax.ShapeDtypeStruct((piece,...  54.4 us
    unnamed x12, local copies, waits for them, and re-layouts  11.2 us

profile of v1, /device:TPU:0, one launch (start us, length us, event | category | flops | bytes accessed | tf_op | source)
XLA Modules:
  0.0 66.3 jit_solution(7458377377146220938)
XLA Ops:
  0.6 54.4 %shard_map.127 = (f32[56,896]{1,0:T(8,128)}, f32[56,896]{1,0:T(8,128)}, f32[448,896]{1,0:T(8,128)}, f32[448,896]{1,0:T(8,128)}, bf16[896,896]{1,0:T(8,128)(2,1)}, /*index=5*/bf16[896,896]{1,0:T(8,128)(2,1)}) custom-call(bf16[1024,896]{1,0:T(8,128)(2,1)} %x_h.1, bf16[1024,896]{1,0:T(8,128)(2,1)} %g_h.1, bf16[896,896]{1,0:T(8,128)(2,1)} %w1_h.1, ...), custom_call_target="tpu_custom_call" | custom-call | flops 6576668672 | bytes 17000000 | tf_op jit(solution)/shard_map/pallas_call | solution.py:507
  55.1 1.6 %copy.20 = f32[56,896]{1,0:T(8,128)} copy(f32[56,896]{1,0:T(8,128)} %get-tuple-element.12) | data formatting | bytes 401408
  56.7 1.6 %copy.21 = f32[56,896]{1,0:T(8,128)} copy(f32[56,896]{1,0:T(8,128)} %get-tuple-element.13) | data formatting | bytes 401408
  58.3 0.0 copy-start.2
  58.3 2.8 %copy.22 = f32[448,896]{1,0:T(8,128)} copy(f32[448,896]{1,0:T(8,128)} %get-tuple-element.14) | data formatting | bytes 3211264
  61.1 0.0 copy-done.2
  61.1 0.0 copy-start.1
  61.1 1.2 %copy.23 = f32[448,896]{1,0:T(8,128)} copy(f32[448,896]{1,0:T(8,128)S(1)} %copy-done.2) | data formatting | bytes 3211264
  62.3 0.8 %copy-done.1 = bf16[896,896]{1,0:T(8,128)(2,1)S(1)} copy-done((bf16[896,896]{1,0:T(8,128)(2,1)S(1)}, bf16[896,896]{1,0:T(8,128)(2,1)}, u32[]{:S(2)}) %copy-start.1) | copy-done | bytes 1605656
  63.1 0.0 copy-start
  63.1 1.2 %copy.24 = bf16[896,896]{1,0:T(8,128)(2,1)} copy(bf16[896,896]{1,0:T(8,128)(2,1)S(1)} %copy-done.1) | data formatting | bytes 3211264
  64.3 0.8 %copy-done = bf16[896,896]{1,0:T(8,128)(2,1)S(1)} copy-done((bf16[896,896]{1,0:T(8,128)(2,1)S(1)}, bf16[896,896]{1,0:T(8,128)(2,1)}, u32[]{:S(2)}) %copy-start) | copy-done | bytes 1605656
  65.1 1.2 %copy.25 = bf16[896,896]{1,0:T(8,128)(2,1)} copy(bf16[896,896]{1,0:T(8,128)(2,1)S(1)} %copy-done) | data formatting | bytes 3211264
Async XLA Ops:
  58.3 2.8 %copy-start.2 = (f32[448,896]{1,0:T(8,128)S(1)}, f32[448,896]{1,0:T(8,128)}, u32[]{:S(2)}) copy-start(f32[448,896]{1,0:T(8,128)} %get-tuple-element.15) | copy-start | bytes 4816900
  61.1 2.0 %copy-start.1 = (bf16[896,896]{1,0:T(8,128)(2,1)S(1)}, bf16[896,896]{1,0:T(8,128)(2,1)}, u32[]{:S(2)}) copy-start(bf16[896,896]{1,0:T(8,128)(2,1)} %get-tuple-element.16) | copy-start | bytes 4816900
  63.1 2.0 %copy-start = (bf16[896,896]{1,0:T(8,128)(2,1)S(1)}, bf16[896,896]{1,0:T(8,128)(2,1)}, u32[]{:S(2)}) copy-start(bf16[896,896]{1,0:T(8,128)(2,1)} %get-tuple-element.17) | copy-start | bytes 4816900

commit v2 on v1

--- a/solution.py
+++ b/solution.py
@@ -116,12 +116,12 @@
     m1_h,
     o2_h,
     m2_h,
-    no1_h,
-    nm1_h,
-    no2_h,
-    nm2_h,
-    r1_h,
-    r2_h,
+    no1,
+    nm1,
+    no2,
+    nm2,
+    rs1,
+    rs2,
     xv,
     gv,
     w1v,
@@ -146,16 +146,8 @@
     own,
     na,
     nb,
-    no1,
-    nm1,
-    no2,
-    nm2,
-    rs1,
-    rs2,
     in_sem,
-    out_sem,
-    out2_sem,
-    rs1_sem,
+    x_sem,
     fs_sem,
     fr_sem,
     as_sem,
@@ -193,21 +185,31 @@
     def plane(other_chip):
         return (row, other_chip * 2 + core)
 
-    loads = {}
-    for i, (name, src, dst) in enumerate(
-        (
-            ("x", x_h, xv),
-            ("w1", w1_h, w1v),
-            ("g", g_h, gv),
-            ("w2", w2_h, w2v),
-            ("o2", o2_h, o2v),
-            ("m2", m2_h, m2v),
-            ("o1", o1_h, o1v),
-            ("m1", m1_h, m1v),
-        )
-    ):
-        loads[name] = pltpu.make_async_copy(src, dst, in_sem.at[i])
-        loads[name].start()
+    tiles = tokens // TOKEN_TILE
+
+    def tile_of(t):
+        return pl.ds(pl.multiple_of(t * TOKEN_TILE, TOKEN_TILE), TOKEN_TILE)
+
+    def load_tokens(t):
+        return pltpu.make_async_copy(x_h.at[tile_of(t)], xv.at[tile_of(t)], x_sem.at[t])
+
+    loads = {
+        name: pltpu.make_async_copy(src, dst, in_sem.at[i])
+        for i, (name, src, dst) in enumerate(
+            (
+                ("w1", w1_h, w1v),
+                ("g", g_h, gv),
+                ("w2", w2_h, w2v),
+                ("o2", o2_h, o2v),
+                ("m2", m2_h, m2v),
+                ("o1", o1_h, o1v),
+                ("m1", m1_h, m1v),
+            )
+        )
+    }
+    loads["w1"].start()
+    for t in range(tiles):
+        load_tokens(t).start()
 
     barrier = pltpu.get_barrier_semaphore()
     pl.semaphore_signal(barrier, inc=1, device_id=across, device_id_type=MESH)
@@ -227,55 +229,79 @@
             device_id_type=MESH,
         )
 
-    loads["x"].wait()
+    mine = row * half
+    theirs = (1 - row) * half
+    first = LANES
+    rest = (half - first) // 2
+
+    def sent_part(sender, i):
+        if i == 0:
+            return (1 - sender) * (half - first), first
+        return sender * first + (i - 1) * rest, rest
+
+    def rows_at(start, size):
+        return pl.ds(pl.multiple_of(start, 16), size)
+
+    def hidden_of(inputs, weight):
+        hidden = jnp.dot(inputs, weight, preferred_element_type=F32) * scale
+        return hidden, jax.nn.sigmoid(hidden)
+
     loads["w1"].wait()
-
-    def forward(t, carry):
-        at = pl.ds(pl.multiple_of(t * TOKEN_TILE, TOKEN_TILE), TOKEN_TILE)
-        inputs = xv[at, :]
-        hidden = jnp.dot(inputs, w1v[...], preferred_element_type=F32) * scale
-        logistic = jax.nn.sigmoid(hidden)
-        st[:, at] = (hidden * logistic).astype(BF16).T
-        dv[at, :] = logistic * (1.0 + hidden * (1.0 - logistic))
-        xt[:, at] = inputs.T
-        return carry
-
-    lax.fori_loop(0, tokens // TOKEN_TILE, forward, 0)
+    start = theirs + sent_part(row, 0)[0]
+    early = pl.ds(pl.multiple_of(start, LANES), first)
+
+    def forward_early(t, carry):
+        load_tokens(t).wait()
+        hidden, logistic = hidden_of(xv[tile_of(t), :], w1v[:, early])
+        st[early, tile_of(t)] = (hidden * logistic).astype(BF16).T
+        return carry
+
+    loads["g"].start()
+    loads["w2"].start()
+    lax.fori_loop(0, tiles, forward_early, 0)
     loads["g"].wait()
     loads["w2"].wait()
+    for name in ("o2", "m2", "o1", "m1"):
+        loads[name].start()
     pl.semaphore_wait(barrier, chips + 1)
-
-    mine = row * half
-    theirs = (1 - row) * half
-
-    def rows_of(base, i):
-        return pl.ds(pl.multiple_of(base + i * chunk, 16), chunk)
 
     def part(i):
         return pl.ds(pl.multiple_of(i * chunk, 16), chunk)
 
-    def final_second(base, i):
-        at = rows_of(base, i)
+    def final_second(at):
         grad = jnp.dot(st[at, :], gv[...], preferred_element_type=F32) * scale
         final = w2v[at, :].astype(F32) - inner_rate * grad
         f2[at, :] = final
         return final
 
     def copy_final(i):
-        return remote(fsend.at[part(i)], frecv.at[part(i)], fs_sem.at[i], fr_sem.at[i], across)
+        at = rows_at(*sent_part(row, i))
+        return remote(fsend.at[at], frecv.at[at], fs_sem.at[i], fr_sem.at[i], across)
 
     def copy_partial(i):
         return remote(asend.at[part(i)], arecv.at[part(i)], as_sem.at[i], ar_sem.at[i], across)
 
-    def send_final(i, carry):
-        fsend[part(i), :] = final_second(theirs, i).astype(BF16)
+    def send_final(i):
+        start, size = sent_part(row, i)
+        fsend[rows_at(start, size), :] = final_second(rows_at(theirs + start, size)).astype(BF16)
         copy_final(i).start()
-        return carry
-
-    lax.fori_loop(0, CHUNKS // 2, send_final, 0)
+
+    send_final(0)
+
+    def forward(t, carry):
+        at = tile_of(t)
+        inputs = xv[at, :]
+        hidden, logistic = hidden_of(inputs, w1v[...])
+        st[:, at] = (hidden * logistic).astype(BF16).T
+        dv[at, :] = logistic * (1.0 + hidden * (1.0 - logistic))
+        xt[:, at] = inputs.T
+        return carry
+
+    lax.fori_loop(0, tiles, forward, 0)
+    send_final(1)
 
     def backward(t, carry):
-        at = pl.ds(pl.multiple_of(t * TOKEN_TILE, TOKEN_TILE), TOKEN_TILE)
+        at = tile_of(t)
         back = (
             lax.dot_general(
                 gv[at, :], w2v[...], (((1,), (1,)), ((), ())), preferred_element_type=F32
@@ -285,7 +311,7 @@
         fc[at, :] = (back * dv[at, :]).astype(BF16)
         return carry
 
-    lax.fori_loop(0, tokens // TOKEN_TILE, backward, 0)
+    lax.fori_loop(0, tiles, backward, 0)
 
     def copy_core(t):
         at = pl.ds(t * 2, 2)
@@ -293,7 +319,20 @@
             f1.at[1 - core, at], r1.at[at], c1s_sem.at[t], c1r_sem.at[t], sibling
         )
 
-    def final_first(t, carry):
+    def copy_sum(owner):
+        return remote(
+            s2.at[owner], r2.at[chip], s2s_sem.at[owner], s2r_sem.at[chip], plane(owner)
+        )
+
+    def chip_sum(owner):
+        return pack_piece(f1[core, owner] + r1[owner], padded)
+
+    def send_sum(owner):
+        s2[owner] = chip_sum(owner).astype(BF16)
+        copy_sum(owner).start()
+
+    def final_first(turn):
+        t = lax.rem(depth + 1 + turn, depths)
         rows = 4 * piece
         at = pl.ds(pl.multiple_of(t * rows, 16), rows)
         grad = jnp.dot(xt[at, :], fc[...], preferred_element_type=F32) * scale
@@ -301,37 +340,30 @@
         for j in range(4):
             f1[j % 2, t * 2 + j // 2] = final[j * piece : (j + 1) * piece]
         copy_core(t).start()
-        return carry
-
-    lax.fori_loop(0, chips // 2, final_first, 0)
-    lax.fori_loop(CHUNKS // 2, CHUNKS, send_final, 0)
-
-    def wait_core(t, carry):
+
+    def pass_sums(turn):
+        t = lax.rem(depth + 1 + turn, depths)
         copy_core(t).wait_recv()
-        return carry
-
-    lax.fori_loop(0, chips // 2, wait_core, 0)
-
-    def copy_sum(d):
-        return remote(
-            s2.at[d], r2.at[chip], s2s_sem.at[d], s2r_sem.at[chip], plane(lax.rem(chip + d, chips))
-        )
-
-    def send_sum(d, carry):
-        owner = lax.rem(chip + d, chips)
-        total = f1[core, owner] + r1[owner]
-        s2[d] = pack_piece(total, padded).astype(BF16)
-        copy_sum(d).start()
-        return carry
-
-    lax.fori_loop(1, chips, send_sum, 0)
-    own[...] = pack_piece(f1[core, chip] + r1[chip], padded)
+        send_sum(t * 2 + side)
+        send_sum(t * 2 + 1 - side)
+
+    def first_turn(turn, carry):
+        final_first(turn)
+        pass_sums(turn - 1)
+        return carry
+
+    final_first(0)
+    lax.fori_loop(1, depths, first_turn, 0)
+    send_final(2)
+    copy_core(depth).wait_recv()
+    send_sum(depth * 2 + 1 - side)
+    own[...] = chip_sum(chip)
 
     loads["o2"].wait()
     loads["m2"].wait()
 
     def send_partial(i, carry):
-        final = final_second(mine, i)
+        final = final_second(rows_at(mine + i * chunk, chunk))
         share, _ = nesterov(o2v[part(i), :], m2v[part(i), :], final, 2)
         asend[part(i), :] = share.astype(BF16)
         copy_partial(i).start()
@@ -339,31 +371,29 @@
 
     lax.fori_loop(0, CHUNKS, send_partial, 0)
 
-    def out_second(i):
-        return (
-            pltpu.make_async_copy(no2.at[part(i)], no2_h.at[part(i)], out2_sem.at[0, i]),
-            pltpu.make_async_copy(nm2.at[part(i)], nm2_h.at[part(i)], out2_sem.at[1, i]),
-            pltpu.make_async_copy(
-                rs2.at[rows_of(mine, i)], r2_h.at[rows_of(mine, i)], out2_sem.at[2, i]
-            ),
-        )
-
-    def out_reset(i):
-        at = rows_of(theirs, i)
-        return pltpu.make_async_copy(rs2.at[at], r2_h.at[at], out2_sem.at[3, i])
-
-    def take_final(i, carry):
-        copy_final(i).wait_recv()
-        summed = f2[rows_of(mine, i), :] + frecv[part(i), :].astype(F32)
-        new_outer, new_moment = nesterov(o2v[part(i), :], m2v[part(i), :], summed, 2)
-        no2[part(i), :] = new_outer
-        nm2[part(i), :] = new_moment
-        rs2[rows_of(mine, i), :] = new_outer.astype(BF16)
-        for copy in out_second(i):
-            copy.start()
-        return carry
-
-    lax.fori_loop(0, CHUNKS, take_final, 0)
+    def take_final(i):
+        start, size = sent_part(1 - row, i)
+        at, there = rows_at(start, size), rows_at(mine + start, size)
+        remote(
+            fsend.at[at], frecv.at[at], fs_sem.at[i], fr_sem.at[i], across
+        ).wait_recv()
+        summed = f2[there, :] + frecv[at, :].astype(F32)
+        new_outer, new_moment = nesterov(o2v[at, :], m2v[at, :], summed, 2)
+        no2[at, :] = new_outer
+        nm2[at, :] = new_moment
+        rs2[there, :] = new_outer.astype(BF16)
+
+    for i in range(3):
+        take_final(i)
+
+    def take_partial(i, carry):
+        copy_partial(i).wait_recv()
+        at = rows_at(theirs + i * chunk, chunk)
+        share = (outer_rate * (1.0 + momentum_coef) / 2) * f2[at, :]
+        rs2[at, :] = (arecv[part(i), :].astype(F32) + share).astype(BF16)
+        return carry
+
+    lax.fori_loop(0, 1, take_partial, 0)
 
     loads["o1"].wait()
     loads["m1"].wait()
@@ -371,7 +401,7 @@
     def take_sum(d, carry):
         source = lax.rem(chip + chips - d, chips)
         remote(
-            s2.at[d], r2.at[source], s2s_sem.at[d], s2r_sem.at[source], plane(source)
+            s2.at[source], r2.at[source], s2s_sem.at[source], s2r_sem.at[source], plane(source)
         ).wait_recv()
         own[...] += r2[source].astype(F32)
         return carry
@@ -382,10 +412,6 @@
     no1[...] = new_outer
     nm1[...] = new_moment
     na[chip] = pack_piece(new_outer, padded).astype(BF16)
-    out_first = (
-        pltpu.make_async_copy(no1, no1_h, out_sem.at[0]),
-        pltpu.make_async_copy(nm1, nm1_h, out_sem.at[1]),
-    )
 
     def copy_depth(d):
         other = lax.rem(depth + d, depths) * 2 + side
@@ -409,18 +435,7 @@
         copy_depth(d).start()
     copy_side(0).start()
     copy_sibling(chip).start()
-    for copy in out_first:
-        copy.start()
-
-    def take_partial(i, carry):
-        copy_partial(i).wait_recv()
-        at = rows_of(theirs, i)
-        share = (outer_rate * (1.0 + momentum_coef) / 2) * f2[at, :]
-        rs2[at, :] = (arecv[part(i), :].astype(F32) + share).astype(BF16)
-        out_reset(i).start()
-        return carry
-
-    lax.fori_loop(0, 2, take_partial, 0)
+    lax.fori_loop(1, 2, take_partial, 0)
 
     def pass_on(d, carry):
         held = lax.rem(depth + d, depths) * 2 + side
@@ -439,10 +454,6 @@
         return carry
 
     lax.fori_loop(0, depths, pass_core, 0)
-
-    def out_module(q):
-        at = pl.ds(pl.multiple_of(q * 2 * piece, 16), 2 * piece)
-        return pltpu.make_async_copy(rs1.at[at], r1_h.at[at], rs1_sem.at[q])
 
     def place(d, carry):
         q = lax.rem(chip + d, chips)
@@ -453,18 +464,16 @@
             [jnp.where(core == 0, here, there), jnp.where(core == 0, there, here)], axis=0
         )
         rs1[pl.ds(pl.multiple_of(q * 2 * piece, 16), 2 * piece), :] = both.astype(BF16)
-        out_module(q).start()
         return carry
 
     lax.fori_loop(0, chips, place, 0)
     lax.fori_loop(CHUNKS - 1, CHUNKS, take_partial, 0)
 
+    for i in range(3):
+        copy_final(i).wait_send()
+
     def drain(i, carry):
-        copy_final(i).wait_send()
         copy_partial(i).wait_send()
-        for copy in out_second(i):
-            copy.wait()
-        out_reset(i).wait()
         return carry
 
     lax.fori_loop(0, CHUNKS, drain, 0)
@@ -473,18 +482,26 @@
         copy_core(t).wait_send()
         return carry
 
-    lax.fori_loop(0, chips // 2, drain_core, 0)
-    for copy in out_first:
-        copy.wait()
+    lax.fori_loop(0, depths, drain_core, 0)
     for d in range(1, chips):
-        copy_sum(d).wait_send()
+        copy_sum(lax.rem(chip + d, chips)).wait_send()
     for d in range(depths):
         copy_side(d).wait_send()
         if d:
             copy_depth(d).wait_send()
     for q in range(chips):
         copy_sibling(q).wait_send()
-        out_module(q).wait()
+
+
+def write_kernel(*refs):
+    count = (len(refs) - 1) // 2
+    copies = [
+        pltpu.make_async_copy(refs[i], refs[count + i], refs[-1].at[i]) for i in range(count)
+    ]
+    for copy in copies:
+        copy.start()
+    for copy in copies:
+        copy.wait()
 
 
 def on_device_fused(
@@ -504,18 +521,20 @@
     padded = -(-piece * (width // LANES) // 16) * 16
     anywhere = pl.BlockSpec(memory_space=pl.ANY)
     dma = pltpu.SemaphoreType.DMA
-    return pl.pallas_call(
+    shapes = (
+        ((piece, width), F32),
+        ((piece, width), F32),
+        ((half, width), F32),
+        ((half, width), F32),
+        ((width, width), BF16),
+        ((width, width), BF16),
+    )
+    held = pl.BlockSpec(memory_space=pltpu.VMEM)
+    results = pl.pallas_call(
         outer_step_kernel,
-        out_shape=(
-            jax.ShapeDtypeStruct((piece, width), F32),
-            jax.ShapeDtypeStruct((piece, width), F32),
-            jax.ShapeDtypeStruct((half, width), F32),
-            jax.ShapeDtypeStruct((half, width), F32),
-            jax.ShapeDtypeStruct((width, width), BF16),
-            jax.ShapeDtypeStruct((width, width), BF16),
-        ),
+        out_shape=tuple(pltpu.VMEM(shape, dtype) for shape, dtype in shapes),
         in_specs=[anywhere] * 8,
-        out_specs=[anywhere] * 6,
+        out_specs=[held] * 6,
         scratch_shapes=[
             pltpu.VMEM((tokens, width), BF16),
             pltpu.VMEM((tokens, width), BF16),
@@ -541,18 +560,10 @@
             pltpu.VMEM((padded, LANES), F32),
             pltpu.VMEM((chips, padded, LANES), BF16),
             pltpu.VMEM((chips, padded, LANES), BF16),
-            pltpu.VMEM((piece, width), F32),
-            pltpu.VMEM((piece, width), F32),
-            pltpu.VMEM((half, width), F32),
-            pltpu.VMEM((half, width), F32),
-            pltpu.VMEM((width, width), BF16),
-            pltpu.VMEM((width, width), BF16),
             dma((8,)),
-            dma((2,)),
-            dma((4, CHUNKS)),
-            dma((chips,)),
-            dma((CHUNKS,)),
-            dma((CHUNKS,)),
+            dma((tokens // TOKEN_TILE,)),
+            dma((3,)),
+            dma((3,)),
             dma((CHUNKS,)),
             dma((CHUNKS,)),
             dma((chips // 2,)),
@@ -566,7 +577,7 @@
             dma((chips,)),
         ],
         compiler_params=pltpu.CompilerParams(
-            collective_id=0, has_side_effects=True, vmem_limit_bytes=60 * 1024 * 1024
+            collective_id=0, has_side_effects=True, vmem_limit_bytes=50 * 1024 * 1024
         ),
         cost_estimate=pl.CostEstimate(
             flops=8 * tokens * width * width,
@@ -583,6 +594,13 @@
         outer_second,
         momentum_second,
     )
+    return pl.pallas_call(
+        write_kernel,
+        out_shape=tuple(jax.ShapeDtypeStruct(shape, dtype) for shape, dtype in shapes),
+        in_specs=[held] * 6,
+        out_specs=[anywhere] * 6,
+        scratch_shapes=[dma((6,))],
+    )(*results)
 
 
 def on_device(mesh):

time: 67.3 us -> 67.7 us (level)
  Pallas kernels: 54.4 us -> 60.3 us
  local copies, waits for them, and re-layouts: 11.2 us -> 6.02 us
    pallas_call x1 -> x2, Pallas kernels: 54.4 us -> 60.3 us  [the longest x1 54.4 us: on_device_fused(): pl.pallas_call(outer_step_kernel, out_shape=tuple((pltpu.VMEM(shape, dtyp...]
    unnamed x12, local copies, waits for them, and re-layouts: 11.2 us -> 6.02 us
where the time goes in v2:
time: 67.7 us; the launch traced here: 67 us
  Pallas kernels  60.3 us (89%)
  local copies, waits for them, and re-layouts  6.02 us (9%)
    pallas_call x1, Pallas kernels, on_device_fused(): pl.pallas_call(outer_step_kernel, out_shape=tuple((pltpu.VMEM(shape, dtyp...  54.4 us
    unnamed x12, local copies, waits for them, and re-layouts  6.02 us
    pallas_call x1, Pallas kernels, on_device_fused(): pl.pallas_call(write_kernel, out_shape=tuple((jax.ShapeDtypeStruct(shape,...  5.96 us

profile of v2, /device:TPU:0, one launch (start us, length us, event | category | flops | bytes accessed | tf_op | source)
XLA Modules:
  0.0 67.0 jit_solution(17424618577678175003)
XLA Ops:
  0.6 54.4 %shard_map.127 = (f32[56,896]{1,0:T(8,128)S(1)}, f32[56,896]{1,0:T(8,128)S(1)}, f32[448,896]{1,0:T(8,128)S(1)}, f32[448,896]{1,0:T(8,128)S(1)}, bf16[896,896]{1,...) custom-call(bf16[1024,896]{1,0:T(8,128)(2,1)} %x_h.1, bf16[1024,896]{1,0:T(8,128)(2,1)} %g_h.1, bf16[896,896]{1,0:T(8,128)(2,1)} %w1_h.1, ...), custom_call_target="tpu_custom_call" | custom-call | flops 6576668672 | bytes 17000000 | tf_op jit(solution)/shard_map/pallas_call | solution.py:533
  55.0 0.0 copy-start
  55.0 1.2 %copy-done = f32[448,896]{1,0:T(8,128)} copy-done((f32[448,896]{1,0:T(8,128)}, f32[448,896]{1,0:T(8,128)S(1)}, u32[]{:S(2)}) %copy-start) | copy-done | bytes 1605656
  56.2 0.0 copy-start.1
  56.2 1.2 %copy-done.1 = f32[448,896]{1,0:T(8,128)} copy-done((f32[448,896]{1,0:T(8,128)}, f32[448,896]{1,0:T(8,128)S(1)}, u32[]{:S(2)}) %copy-start.1) | copy-done | bytes 1605656
  57.3 0.0 copy-start.2
  57.3 1.2 %copy-done.2 = bf16[896,896]{1,0:T(8,128)(2,1)} copy-done((bf16[896,896]{1,0:T(8,128)(2,1)}, bf16[896,896]{1,0:T(8,128)(2,1)S(1)}, u32[]{:S(2)}) %copy-start.2) | copy-done | bytes 1605656
  58.5 0.0 copy-start.3
  58.5 1.2 %copy-done.3 = bf16[896,896]{1,0:T(8,128)(2,1)} copy-done((bf16[896,896]{1,0:T(8,128)(2,1)}, bf16[896,896]{1,0:T(8,128)(2,1)S(1)}, u32[]{:S(2)}) %copy-start.3) | copy-done | bytes 1605656
  59.7 0.0 copy-start.4
  59.7 0.7 %copy-done.4 = f32[56,896]{1,0:T(8,128)} copy-done((f32[56,896]{1,0:T(8,128)}, f32[56,896]{1,0:T(8,128)S(1)}, u32[]{:S(2)}) %copy-start.4) | copy-done | bytes 200728
  60.4 0.0 copy-start.5
  60.4 0.7 %copy-done.5 = f32[56,896]{1,0:T(8,128)} copy-done((f32[56,896]{1,0:T(8,128)}, f32[56,896]{1,0:T(8,128)S(1)}, u32[]{:S(2)}) %copy-start.5) | copy-done | bytes 200728
  61.0 6.0 %shard_map.128 = (f32[56,896]{1,0:T(8,128)}, f32[56,896]{1,0:T(8,128)}, f32[448,896]{1,0:T(8,128)}, f32[448,896]{1,0:T(8,128)}, bf16[896,896]{1,0:T(8,128)(2,1)}, /*index=5*/bf16[896,896]{1,0:T(8,128)(2,1)}) custom-call(f32[56,896]{1,0:T(8,128)} %copy-done.4, f32[56,896]{1,0:T(8,128)} %copy-done.5, f32[448,896]{1,0:T(8,128)} %copy-done, ...), custom_call_target="tpu_custom_call" | custom-call | tf_op jit(solution)/shard_map/pallas_call | solution.py:597
Async XLA Ops:
  55.0 1.2 %copy-start = (f32[448,896]{1,0:T(8,128)}, f32[448,896]{1,0:T(8,128)S(1)}, u32[]{:S(2)}) copy-start(f32[448,896]{1,0:T(8,128)S(1)} %get-tuple-element.14.refs_2_) | copy-start | bytes 4816900
  56.2 1.2 %copy-start.1 = (f32[448,896]{1,0:T(8,128)}, f32[448,896]{1,0:T(8,128)S(1)}, u32[]{:S(2)}) copy-start(f32[448,896]{1,0:T(8,128)S(1)} %get-tuple-element.15.refs_3_) | copy-start | bytes 4816900
  57.3 1.2 %copy-start.2 = (bf16[896,896]{1,0:T(8,128)(2,1)}, bf16[896,896]{1,0:T(8,128)(2,1)S(1)}, u32[]{:S(2)}) copy-start(bf16[896,896]{1,0:T(8,128)(2,1)S(1)} %get-tuple-element.16.refs_4_) | copy-start | bytes 4816900
  58.5 1.2 %copy-start.3 = (bf16[896,896]{1,0:T(8,128)(2,1)}, bf16[896,896]{1,0:T(8,128)(2,1)S(1)}, u32[]{:S(2)}) copy-start(bf16[896,896]{1,0:T(8,128)(2,1)S(1)} %get-tuple-element.17.refs_5_) | copy-start | bytes 4816900
  59.7 0.7 %copy-start.4 = (f32[56,896]{1,0:T(8,128)}, f32[56,896]{1,0:T(8,128)S(1)}, u32[]{:S(2)}) copy-start(f32[56,896]{1,0:T(8,128)S(1)} %get-tuple-element.12.refs_0_) | copy-start | bytes 602116
  60.4 0.7 %copy-start.5 = (f32[56,896]{1,0:T(8,128)}, f32[56,896]{1,0:T(8,128)S(1)}, u32[]{:S(2)}) copy-start(f32[56,896]{1,0:T(8,128)S(1)} %get-tuple-element.13.refs_1_) | copy-start | bytes 602116
